TPU v7x, 128 devices: a whole 4x4x4 slice. The times are simulated.
128 devices in a mesh: section: 4 (over x_hi, core), dp: 32 (over z, x_lo, y).
Axes of the slice: x: 4 (x_hi: 2, x_lo: 2; x = x_hi * 2 + x_lo), y: 4, z: 4, core: 2. Of those that a mesh axis runs over, the one named last changes fastest.
Arguments:
- factor_rows: bfloat16 [1, 4, 6144, 3072], P(None, 'section', 'dp'), may hold values from -50.4 to 50.4
- entry_rows: bfloat16 [1, 6144, 3072], P(None, 'dp'), may hold values from -50.4 to 50.4
Outputs:
- diagonal_blocks: bfloat16 [1, 4, 3072, 3072], P(None, 'section', 'dp')
- adjacent_blocks: bfloat16 [1, 4, 3072, 3072], P(None, 'section', 'dp')
All inputs are finite; a program needn't handle non-finite values.
Results may differ from a plain program's by a relative error of at most 0.001.
Values may be sent and summed in bfloat16 or wider, within the bound.
A program may use at most 128 MiB of HBM per device.

v0:
```python
import jax
import jax.numpy as jnp
from jax import lax
from jax.sharding import PartitionSpec as P


def shifted(array, axis, by):
    peers = lax.axis_size(axis)
    pairs = [(i, i + by) for i in range(peers) if 0 <= i + by < peers]
    return lax.ppermute(array, axis, pairs)


def products(left_rows, right_rows):
    return jnp.einsum("fjtw,fjtd->fjwd", left_rows, right_rows, preferred_element_type=jnp.float32)


def on_device(factor_rows, entry_rows):
    groups = lax.axis_size("dp")
    owned_width = factor_rows.shape[3] // groups
    first_column = lax.axis_index("dp") * owned_width
    inverse = 1.0 / (factor_rows.shape[2] * groups)
    finale = factor_rows[:, -1]
    arrived = shifted(finale, "section", 1)
    arrived = jnp.where(lax.axis_index("section") == 0, entry_rows, arrived)
    earlier = lax.all_to_all(arrived, "dp", split_axis=2, concat_axis=1, tiled=True)
    pieces = lax.all_gather(factor_rows, "dp", axis=2, tiled=True)
    columns = lax.dynamic_slice_in_dim(pieces, first_column, owned_width, 3)
    left_rows = jnp.concatenate([earlier[:, None], columns[:, :-1]], axis=1)
    diagonal = products(columns, pieces)
    adjacent = products(left_rows, pieces)
    return ((diagonal * inverse).astype(jnp.bfloat16), (adjacent * inverse).astype(jnp.bfloat16))


def solution(mesh):
    placed = (P(None, "section", "dp", None), P(None, "dp", None))
    return jax.shard_map(
        on_device,
        mesh=mesh,
        in_specs=placed,
        out_specs=(P(None, "section", "dp", None), P(None, "section", "dp", None)),
        check_vma=False,
    )
```

profile of v0, /device:TPU:59, one launch (start us, length us, event | category | flops | bytes accessed | tf_op | source)
XLA Modules:
  0.0 497.3 jit_solution(3484402882403127848)
XLA Ops:
  7.2 0.0 copy-start
  7.2 0.0 all-gather.2.cloned.1.call-start
  7.2 0.7 all-gather.2.cloned.1.call-update
  7.9 0.5 copy-done
  8.4 4.3 collective-permute-start
  12.8 24.3 %collective-permute-done = bf16[1,192,3072]{2,1,0:T(8,128)(2,1)S(1)} collective-permute-done((bf16[1,192,3072]{2,1,0:T(8,128)(2,1)S(1)}, bf16[1,192,3072]{2,1,0:T(8,128)(2,1)S(1)}, u32[]{:S(2)}, u32[]{:S(2)}) %collective-permute-start) | collective-permute-done | bytes 1179680 | tf_op jit(solution)/shard_map/ppermute | solution.py:10
  37.0 1.2 broadcast_select_fusion
  38.2 7.6 %copy.8 = bf16[1,192,3072]{1,0,2:T(2,128)(2,1)S(1)} copy(bf16[1,192,3072]{2,1,0:T(8,128)(2,1)} %broadcast_select_fusion) | data formatting | bytes 2359296 | tf_op jit(solution)/shard_map/jit(_where)/select_n | solution.py:24
  45.8 0.5 broadcast.8
  46.3 18.3 %reduce = bf16[3072,192]{1,0:T(8,128)(2,1)} reduce(bf16[3072,1,192]{2,1,0:T(2,128)(2,1)S(1)} %bitcast.33, bf16[]{:T(256)} %broadcast.8), dimensions={1}, to_apply=%bitcast.30.reduce_sub_computation | reduce | bytes 2359298
  64.5 4.5 reshape.25
  69.0 11.3 %all-to-all-start = ((bf16[32,2,9216]{2,1,0:T(2,128)(2,1)}), bf16[32,2,9216]{2,1,0:T(2,128)(2,1)}, u32[]{:S(2)}, u32[]{:S(2)}) async-start(bf16[32,2,9216]{2,1,0:T(2,128)(2,1)} %reshape.25), calls=%async_computation | async-start | bytes 2359296 | tf_op jit(solution)/shard_map/all_to_all | solution.py:25
  80.3 354.9 %all-to-all-done = bf16[32,2,9216]{2,1,0:T(2,128)(2,1)} async-done(((bf16[32,2,9216]{2,1,0:T(2,128)(2,1)}), bf16[32,2,9216]{2,1,0:T(2,128)(2,1)}, u32[]{:S(2)}, u32[]{:S(2)}) %all-to-all-start) | async-done | bytes 1179680 | tf_op jit(solution)/shard_map/all_to_all | solution.py:25
  435.2 9.0 %reshape.26 = bf16[3072,1,192]{2,1,0:T(2,128)(2,1)S(1)} reshape(bf16[32,2,9216]{2,1,0:T(2,128)(2,1)} %all-to-all-done) | data formatting | bytes 2359296
  444.2 6.1 %copy.9 = bf16[1,192,3072]{2,1,0:T(8,128)(2,1)} copy(bf16[1,192,3072]{1,0,2:T(2,128)(2,1)S(1)} %bitcast.34) | data formatting | bytes 2359296 | tf_op jit(solution)/shard_map/all_to_all | solution.py:25
  450.3 2.9 all_to_all.12
  453.2 3.0 copy.10
  456.3 1.7 reshape.24
  458.0 0.0 all-gather.2.cloned.1.call-done
  458.0 16.7 %fusion.16 = bf16[1,1,96,3072]{3,2,1,0:T(8,128)(2,1)} fusion(bf16[1,1,6144,3072]{3,2,1,0:T(8,128)(2,1)} %all-gather.2.cloned.1.call-done, s32[]{:T(128)S(6)} %select_n.11), kind=kOutput, calls=%fused_computation.8 | convolution fusion | flops 3624468480 | bytes 39911428 | tf_op jit(solution)/shard_map/fjtw,fjtd->fjwd/dot_general | solution.py:14
  474.8 15.7 %fusion.19 = bf16[1,1,96,3072]{3,2,1,0:T(8,128)(2,1)} fusion(bf16[6144,96]{0,1:T(8,128)(2,1)S(1)} %reshape.24, bf16[1,1,6144,3072]{3,2,1,0:T(8,128)(2,1)} %all-gather.2.cloned.1.call-done), kind=kOutput, calls=%fused_computation.9 | convolution fusion | flops 3624468480 | bytes 39518208 | tf_op jit(solution)/shard_map/fjtw,fjtd->fjwd/dot_general | solution.py:14
Async XLA Ops:
  7.2 1.3 copy-start
  7.2 450.8 %all-gather.2.cloned.1.call-start = ((), (), s32[]{:S(2)}) async-start(), calls=%async_computation.1 | async-start | bytes 38928384 | tf_op jit(solution)/shard_map/all_gather | solution.py:26
  8.4 28.6 %collective-permute-start = (bf16[1,192,3072]{2,1,0:T(8,128)(2,1)S(1)}, bf16[1,192,3072]{2,1,0:T(8,128)(2,1)S(1)}, u32[]{:S(2)}, u32[]{:S(2)}) collective-permute-start(bf16[1,192,3072]{2,1,0:T(8,128)(2,1)S(1)} %bitcast.36), channel_id=1, source_target_pairs={{0,32},{32,64},{64,96},{1,33},{33,65},{65,97},{2,34},{34,66},{66,9... | collective-permute-start | bytes 3538952 | tf_op jit(solution)/shard_map/ppermute | solution.py:10
  69.0 366.2 %all-to-all-start = ((bf16[32,2,9216]{2,1,0:T(2,128)(2,1)}), bf16[32,2,9216]{2,1,0:T(2,128)(2,1)}, u32[]{:S(2)}, u32[]{:S(2)}) async-start(bf16[32,2,9216]{2,1,0:T(2,128)(2,1)} %reshape.25), calls=%async_computation | async-start | bytes 2359296 | tf_op jit(solution)/shard_map/all_to_all | solution.py:25
Sparse Core Ops, SparseCore 0:
  9.7 426.1 all-gather.1
where the time goes:
time: 498 us; the launch traced here: 497 us
  waiting for transfers between devices  380 us (76%)
  local copies, waits for them, and re-layouts  35.8 us (7%)
  matrix products  32.5 us (7%)
  other arithmetic  19.4 us (4%)
  starting transfers between devices  15.6 us (3%)
  between operations  14.1 us (3%)
    all_to_all x1, waiting for transfers between devices, on_device(): lax.all_to_all(arrived, 'dp', split_axis=2, concat_axis=1, tiled=True)  355 us
    dot_general x2, matrix products, products(): jnp.einsum('fjtw,fjtd->fjwd', left_rows, right_rows, preferred_element_ty...  32.5 us
    ppermute x1, waiting for transfers between devices, shifted(): return lax.ppermute(array, axis, pairs)  24.3 us
    unnamed x1, other arithmetic  18.3 us
    unnamed x5, local copies, waits for them, and re-layouts  14.5 us
    all_to_all x3, local copies, waits for them, and re-layouts, on_device(): lax.all_to_all(arrived, 'dp', split_axis=2, concat_axis=1, tiled=True)  12 us
    all_to_all x1, starting transfers between devices, on_device(): lax.all_to_all(arrived, 'dp', split_axis=2, concat_axis=1, tiled=True)  11.3 us
  transfers between devices with their start and end apart: 3, of which 2 were waited for; matrix products, arithmetic and copies ran while one was open for 10% of the time, Pallas kernels for 0%

commit v1 on v0

v1 whole, which is shorter than its diff:
```python
import functools

import jax
import jax.numpy as jnp
from jax import lax
from jax.experimental import pallas as pl
from jax.experimental.pallas import tpu as pltpu
from jax.sharding import PartitionSpec as P

MESH = pl.DeviceIdType.MESH
RING = 4
ROWS = 192
BLOCK = 768
HALF = 384
SUB = 256
SUBS = BLOCK // SUB
OWNED = 96
PIECES = (0, 1, 3, 2)
FORWARD = ((-1, 0), (1, 3), (-1, 1), (1, 2))


def device(x_hi, x_lo, y, z, core):
    return (x_hi * 2 + core, z * 8 + x_lo * 4 + y)


def turn(position, by):
    return lax.rem(position + by + RING, RING)


def kernel(
    inverse, x_ref, e_ref, d_ref, a_ref, left, right, prev, sent, got, kept, rounded,
    left_send, left_recv, right_send, right_recv, prev_send, prev_recv, pass_send, local_sem,
    x_send, x_recv, out_send, out_recv,
):
    section = lax.axis_index("section")
    group = lax.axis_index("dp")
    x_hi, core = section // 2, lax.rem(section, 2)
    z, x_lo, y = group // 8, lax.rem(group // 4, 2), lax.rem(group, 4)
    here = functools.partial(device, x_hi, x_lo)
    x_partner = device(x_hi, 1 - x_lo, y, z, core)
    other_core = device(x_hi, x_lo, y, z, 1 - core)

    barrier = pltpu.get_barrier_semaphore()

    def greet(target):
        pl.semaphore_signal(barrier, inc=1, device_id=target, device_id_type=MESH)

    for step in range(1, RING):
        greet(here(turn(y, step), z, core))
        greet(here(y, turn(z, step), core))
    greet(x_partner)
    greet(other_core)
    expected = 8

    @pl.when(core == 0)
    def _():
        for step in range(RING):
            @pl.when((z != y) | (step != 0))
            def _():
                greet(here(z, turn(z, step), core))

        @pl.when(x_hi == 1)
        def _():
            for row in range(RING):
                greet(device(0, x_lo, row, z, 1))

    expected = expected + jnp.where(
        core == 0, jnp.where(z == y, 3, 4), jnp.where(x_hi == 0, 4, 0)
    )
    pl.semaphore_wait(barrier, expected)

    def remote(src, dst, send, recv, target):
        return pltpu.make_async_remote_copy(
            src_ref=src, dst_ref=dst, send_sem=send, recv_sem=recv, device_id=target, device_id_type=MESH
        )

    def slot(row_z, row_y):
        return row_z * RING + row_y

    def piece(buffer, index):
        return buffer.at[pl.ds(pl.multiple_of(index * ROWS, ROWS), ROWS)]

    def columns(ref, index):
        return ref.at[:, pl.ds(pl.multiple_of(index * BLOCK, BLOCK), BLOCK)]

    mine = slot(z, y)

    class Flow:
        def __init__(self, buffer, send, recv, along_z):
            self.buffer, self.send, self.recv, self.along_z = buffer, send, recv, along_z
            self.count = 0
            self.copies = []

        def start(self, src, index, target):
            copy = remote(src, piece(self.buffer, index), self.send.at[self.count], self.recv.at[index], target)
            copy.start()
            self.count += 1
            self.copies.append(copy)

        def wait(self, index):
            whole = piece(self.buffer, index)
            remote(whole, whole, self.send.at[0], self.recv.at[index], x_partner).wait_recv()

        def spread(self, src):
            for step in (1, 3, 2):
                if self.along_z:
                    to = turn(y, step)
                    target = here(to, z, core)
                else:
                    to = turn(z, step)
                    target = here(y, to, core)
                self.start(columns(src, to), mine, target)

        def keep(self, src, sem):
            own = y if self.along_z else z
            copy = pltpu.make_async_copy(columns(src, own), piece(self.buffer, mine), self.recv.at[mine])
            copy.start()

        def index(self, step, part):
            if self.along_z:
                return slot(turn(z, step), turn(y, part))
            return slot(turn(z, part), turn(y, step))

        def neighbour(self, step):
            return here(y, turn(z, step), core) if self.along_z else here(turn(y, step), z, core)

        def push(self, index, step):
            self.start(piece(self.buffer, index), index, self.neighbour(step))

        def own(self, part):
            index = self.index(0, part)
            self.wait(index)
            self.push(index, 1)
            self.push(index, -1)
            return index

        def relay(self, step, part):
            index = self.index(step, part)
            self.wait(index)
            self.push(index, -step)
            return index

        def rest(self):
            return [self.index(s, p) for s, ps in ((-1, (3, 2)), (1, (0, 1)), (2, PIECES)) for p in ps]

    def product(lhs, rhs, half, sub):
        start = pl.multiple_of(half * HALF, HALF)
        return lax.dot_general(
            lhs[:, pl.ds(start, HALF)],
            rhs[:, pl.ds(pl.multiple_of(sub * SUB, SUB), SUB)],
            (((0,), (0,)), ((), ())),
            preferred_element_type=jnp.float32,
        )

    def x_copy(which, sub):
        return remote(
            sent.at[which, sub], got.at[which, sub], x_send.at[which, sub], x_recv.at[which, sub], x_partner
        )

    def partner_half(which, lhs, rhs):
        @pl.loop(0, SUBS)
        def _(sub):
            sent[which, sub] = product(lhs, rhs, 1 - x_lo, sub)
            x_copy(which, sub).start()

    def own_half(which, lhs, rhs):
        @pl.loop(0, SUBS)
        def _(sub):
            kept[which, sub] = product(lhs, rhs, x_lo, sub)

    def out_copy(which, out, turned, sub, owner, start):
        block, row_z = (z, y) if turned else (y, z)
        src = rounded.at[which, sub, pl.ds(owner * OWNED, OWNED)]
        dst = out.at[:, pl.ds(pl.multiple_of(block * BLOCK + sub * SUB, SUB), SUB)]
        recv = out_recv.at[which, block, sub]
        itself = (owner == y) & (row_z == z)

        @pl.when(itself)
        def _():
            if start:
                pltpu.make_async_copy(src, dst, recv).start()

        @pl.when(jnp.logical_not(itself))
        def _():
            copy = remote(src, dst, out_send.at[which, sub, owner], recv, here(owner, row_z, core))
            if start:
                copy.start()
            else:
                copy.wait_send()

    def finish(which, out, turned):
        @pl.loop(0, SUBS)
        def _(sub):
            x_copy(which, sub).wait_recv()
            rounded[which, sub] = ((kept[which, sub] + got[which, sub]) * inverse).astype(jnp.bfloat16)
            for owner in range(RING):
                out_copy(which, out, turned, sub, owner, True)

    def drain(which, out, turned):
        @pl.loop(0, SUBS)
        def _(sub):
            x_copy(which, sub).wait_send()
            for owner in range(RING):
                out_copy(which, out, turned, sub, owner, False)
            for block in range(RING):
                dst = out.at[:, pl.ds(pl.multiple_of(block * BLOCK + sub * SUB, SUB), SUB)]
                remote(
                    rounded.at[which, sub, pl.ds(0, OWNED)], dst, out_send.at[which, sub, 0],
                    out_recv.at[which, block, sub], x_partner,
                ).wait_recv()

    @pl.when(core == 0)
    def _():
        lefts = Flow(left, left_send, left_recv, False)
        rights = Flow(right, right_send, right_recv, True)
        prevs = Flow(prev, prev_send, prev_recv, True)
        passed = []

        def hand_over(index):
            copy = remote(piece(left, index), piece(prev, index), pass_send.at[len(passed)], prev_recv.at[index], other_core)
            copy.start()
            passed.append(copy)

        lefts.keep(x_ref, local_sem)
        rights.keep(x_ref, local_sem)
        lefts.spread(x_ref)
        rights.spread(x_ref)
        for part in PIECES:
            hand_over(lefts.own(part))
            rights.own(part)

        @pl.when(x_hi == 0)
        def _():
            prevs.keep(e_ref, local_sem)
            prevs.spread(e_ref)
        first = list(prevs.copies)
        prevs.copies = []

        for step, part in FORWARD:
            hand_over(lefts.relay(step, part))
            rights.relay(step, part)
        for part in PIECES:
            prevs.own(part)
        for index in lefts.rest():
            lefts.wait(index)
            hand_over(index)
        for index in rights.rest():
            rights.wait(index)
        partner_half(0, left, right)
        for step, part in FORWARD[:2]:
            prevs.relay(step, part)
        own_half(0, left, right)
        for step, part in FORWARD[2:]:
            prevs.relay(step, part)
        finish(0, d_ref, False)
        for index in prevs.rest():
            prevs.wait(index)
        partner_half(1, prev, left)
        own_half(1, prev, left)
        finish(1, a_ref, True)
        drain(0, d_ref, False)
        drain(1, a_ref, True)
        for copy in lefts.copies + rights.copies + prevs.copies + passed:
            copy.wait_send()

        @pl.when(x_hi == 0)
        def _():
            for count, _ in enumerate(first):
                remote(piece(prev, mine), piece(prev, mine), prev_send.at[count], prev_recv.at[mine], x_partner).wait_send()

    @pl.when(core == 1)
    def _():
        lefts = Flow(left, left_send, left_recv, False)
        rights = Flow(right, right_send, right_recv, True)
        prevs = Flow(prev, prev_send, prev_recv, False)
        lefts.keep(x_ref, local_sem)
        rights.keep(x_ref, local_sem)
        lefts.spread(x_ref)
        rights.spread(x_ref)

        def relayed(to):
            return remote(
                columns(x_ref, to), piece(prev, mine), prev_send.at[to], prev_recv.at[mine], device(1, x_lo, to, z, 0)
            )

        @pl.when(x_hi == 0)
        def _():
            for to in range(RING):
                relayed(to).start()

        for part in PIECES:
            prevs.wait(prevs.index(0, part))
        for part in PIECES:
            lefts.own(part)
            rights.own(part)
        for step, part in FORWARD:
            lefts.relay(step, part)
            rights.relay(step, part)
        for step, part in FORWARD:
            prevs.wait(prevs.index(step, part))
        for index in prevs.rest():
            prevs.wait(index)
        for index in rights.rest():
            rights.wait(index)
        partner_half(1, prev, right)
        own_half(1, prev, right)
        for index in lefts.rest():
            lefts.wait(index)
        partner_half(0, left, right)
        own_half(0, left, right)
        finish(1, a_ref, False)
        finish(0, d_ref, False)
        drain(1, a_ref, False)
        drain(0, d_ref, False)
        for copy in lefts.copies + rights.copies:
            copy.wait_send()

        @pl.when(x_hi == 0)
        def _():
            for to in range(RING):
                relayed(to).wait_send()


def on_device(factor_rows, entry_rows):
    rows, width = factor_rows.shape[2:]
    tokens = rows * lax.axis_size("dp")
    out = jax.ShapeDtypeStruct((OWNED, width), jnp.bfloat16)
    block = pltpu.VMEM((tokens // 2, BLOCK), jnp.bfloat16)
    part = pltpu.VMEM((2, SUBS, HALF, SUB), jnp.float32)
    slots = pltpu.SemaphoreType.DMA((16,))
    diagonal, adjacent = pl.pallas_call(
        functools.partial(kernel, 1.0 / tokens),
        out_shape=(out, out),
        in_specs=[pl.BlockSpec(memory_space=pl.ANY)] * 2,
        out_specs=[pl.BlockSpec(memory_space=pl.ANY)] * 2,
        scratch_shapes=[block, block, block, part, part, part, pltpu.VMEM((2, SUBS, HALF, SUB), jnp.bfloat16)]
        + [slots] * 7
        + [
            pltpu.SemaphoreType.DMA,
            pltpu.SemaphoreType.DMA((2, SUBS)),
            pltpu.SemaphoreType.DMA((2, SUBS)),
            pltpu.SemaphoreType.DMA((2, SUBS, RING)),
            pltpu.SemaphoreType.DMA((2, RING, SUBS)),
        ],
        compiler_params=pltpu.CompilerParams(
            collective_id=0, has_side_effects=True, vmem_limit_bytes=60 * 2**20
        ),
        cost_estimate=pl.CostEstimate(flops=4 * BLOCK * BLOCK * tokens // 2, bytes_accessed=2**22, transcendentals=0),
        name="blocks",
    )(factor_rows.reshape(rows, width), entry_rows.reshape(rows, width))
    return diagonal.reshape(1, 1, OWNED, width), adjacent.reshape(1, 1, OWNED, width)


def solution(mesh):
    placed = (P(None, "section", "dp", None), P(None, "dp", None))
    return jax.shard_map(
        on_device,
        mesh=mesh,
        in_specs=placed,
        out_specs=(P(None, "section", "dp", None), P(None, "section", "dp", None)),
        check_vma=False,
    )
```

time: 498 us -> 131 us (0.26)
  the two profiles are of different devices: /device:TPU:59 before, /device:TPU:20 now
where the time goes in v1:
time: 131 us
  Pallas kernels  127 us (97%)
  local copies, waits for them, and re-layouts  2.8 us (2%)
    pallas_call x1, Pallas kernels, on_device(): pl.pallas_call(functools.partial(kernel, 1.0 / tokens), out_shape=(out, o...  127 us
    unnamed x4, local copies, waits for them, and re-layouts  2.8 us

profile of v1, /device:TPU:20, one launch (start us, length us, event | category | flops | bytes accessed | tf_op | source)
XLA Modules:
  0.0 130.9 jit_solution(3018871400636019216)
XLA Ops:
  0.6 127.4 %blocks.1 = (bf16[96,3072]{1,0:T(8,128)(2,1)}, bf16[96,3072]{1,0:T(8,128)(2,1)}) custom-call(bf16[192,3072]{1,0:T(8,128)(2,1)} %bitcast.6, bf16[192,3072]{1,0:T(8,128)(2,1)} %bitcast.7), custom_call_target="tpu_custom_call" | custom-call | flops 7247757312 | bytes 4194304 | tf_op jit(solution)/shard_map/blocks/pallas_call | solution.py:331
  128.1 0.0 copy-start
  128.1 2.0 %copy.6 = bf16[1,1,96,3072]{3,2,1,0:T(8,128)(2,1)} copy(bf16[1,1,96,3072]{3,2,1,0:T(8,128)(2,1)} %bitcast.5) | data formatting | bytes 1179648
  130.1 0.0 copy-done
  130.1 0.8 copy.7
Async XLA Ops:
  128.1 2.0 %copy-start = (bf16[96,3072]{1,0:T(8,128)(2,1)S(1)}, bf16[96,3072]{1,0:T(8,128)(2,1)}, u32[]{:S(2)}) copy-start(bf16[96,3072]{1,0:T(8,128)(2,1)} %get-tuple-element.5) | copy-start | bytes 1769476

commit v2 on v0

v2 whole, which is shorter than its diff:
```python
import functools

import jax
import jax.numpy as jnp
from jax import lax
from jax.experimental import pallas as pl
from jax.experimental.pallas import tpu as pltpu
from jax.sharding import PartitionSpec as P

MESH = pl.DeviceIdType.MESH
RING = 4
ROWS = 192
BLOCK = 768
HALF = 384
OWNED = 96
DEPTH = 3
PIECES = (0, 1, 3, 2)
FORWARD = ((-1, 0), (1, 3), (-1, 1), (1, 2))


def device(x_hi, x_lo, y, z, core):
    return (x_hi * 2 + core, z * 8 + x_lo * 4 + y)


def turn(position, by):
    return lax.rem(position + by + RING, RING)


def remote(src, dst, send, recv, target):
    return pltpu.make_async_remote_copy(
        src_ref=src, dst_ref=dst, send_sem=send, recv_sem=recv, device_id=target, device_id_type=MESH
    )


def slot(row_z, row_y):
    return row_z * RING + row_y


class Flow:
    def __init__(self, place, buffer, send, recv, along_z, halves):
        self.here, self.y, self.z = place
        self.buffer, self.send, self.recv, self.along_z, self.halves = buffer, send, recv, along_z, halves
        self.copies = ([], [])
        self.flying = {1: [], -1: []}
        self.mine = slot(self.z, self.y)

    def piece(self, order, index):
        return self.buffer.at[self.halves[order], pl.ds(pl.multiple_of(index * ROWS, ROWS), ROWS)]

    def columns(self, src, order, block):
        start = pl.multiple_of(block * BLOCK + self.halves[order] * HALF, HALF)
        return src.at[:, pl.ds(start, HALF)]

    def start(self, src, order, index, target):
        half = self.halves[order]
        count = len(self.copies[order])
        copy = remote(src, self.piece(order, index), self.send.at[half, count], self.recv.at[half, index], target)
        copy.start()
        self.copies[order].append(copy)

    def wait(self, order, index):
        whole = self.piece(order, index)
        half = self.halves[order]
        remote(whole, whole, self.send.at[half, 0], self.recv.at[half, index], self.neighbour(1)).wait_recv()

    def spread(self, src, order):
        own = self.y if self.along_z else self.z
        pltpu.make_async_copy(
            self.columns(src, order, own), self.piece(order, self.mine), self.recv.at[self.halves[order], self.mine]
        ).start()
        for step in (1, 3, 2):
            to = turn(own, step)
            target = self.here(to, self.z) if self.along_z else self.here(self.y, to)
            self.start(self.columns(src, order, to), order, self.mine, target)

    def index(self, step, part):
        if self.along_z:
            return slot(turn(self.z, step), turn(self.y, part))
        return slot(turn(self.z, part), turn(self.y, step))

    def neighbour(self, step):
        return self.here(self.y, turn(self.z, step)) if self.along_z else self.here(turn(self.y, step), self.z)

    def push(self, order, index, step):
        flying = self.flying[step]
        if len(flying) == DEPTH:
            past, count = flying.pop(0)
            self.copies[past][count].wait_send()
            self.copies[past][count] = None
        flying.append((order, len(self.copies[order])))
        self.start(self.piece(order, index), order, index, self.neighbour(step))

    def own(self, order, part):
        index = self.index(0, part)
        self.wait(order, index)
        self.push(order, index, 1)
        self.push(order, index, -1)
        return index

    def relay(self, order, step, part):
        index = self.index(step, part)
        self.wait(order, index)
        self.push(order, index, -step)
        return index

    REST = ((-1, 3), (-1, 2), (1, 0), (1, 1), (2, 0), (2, 1), (2, 3), (2, 2))

    def rest(self):
        return [self.index(step, part) for step, part in self.REST]

    def wait_rest(self, order):
        for index in self.rest():
            self.wait(order, index)

    def drain(self, order, first=0):
        for copy in self.copies[order][first:]:
            if copy is not None:
                copy.wait_send()


def weave(relay, behind, own, ahead):
    relay(behind, *FORWARD[0])
    relay(behind, *FORWARD[1])
    own(ahead, 0)
    own(ahead, 1)
    relay(behind, *FORWARD[2])
    relay(behind, *FORWARD[3])
    own(ahead, 3)
    own(ahead, 2)


def kernel(
    inverse, x_ref, e_ref, d_ref, a_ref, left, right, prev, sent, got, kept, rounded,
    left_send, left_recv, right_send, right_recv, prev_send, prev_recv, pass_send,
    x_send, x_recv, out_send, out_recv,
):
    section = lax.axis_index("section")
    group = lax.axis_index("dp")
    x_hi, core = section // 2, lax.rem(section, 2)
    z, x_lo, y = group // 8, lax.rem(group // 4, 2), lax.rem(group, 4)

    def here(at_y, at_z):
        return device(x_hi, x_lo, at_y, at_z, core)

    place = (here, y, z)
    theirs, ours = 1 - x_lo, x_lo
    x_partner = device(x_hi, 1 - x_lo, y, z, core)
    other_core = device(x_hi, x_lo, y, z, 1 - core)

    barrier = pltpu.get_barrier_semaphore()

    def greet(target):
        pl.semaphore_signal(barrier, inc=1, device_id=target, device_id_type=MESH)

    for step in range(1, RING):
        greet(here(turn(y, step), z))
        greet(here(y, turn(z, step)))
    greet(x_partner)
    greet(other_core)

    @pl.when(core == 0)
    def _():
        for step in range(RING):
            @pl.when((z != y) | (step != 0))
            def _():
                greet(here(z, turn(z, step)))

        @pl.when(x_hi == 1)
        def _():
            for row in range(RING):
                greet(device(0, x_lo, row, z, 1))

    expected = 8 + jnp.where(core == 0, jnp.where(z == y, 3, 4), jnp.where(x_hi == 0, 4, 0))
    pl.semaphore_wait(barrier, expected)

    def product(lhs, rhs, row_half, column_half):
        return lax.dot_general(
            lhs[row_half], rhs[column_half], (((0,), (0,)), ((), ())), preferred_element_type=jnp.float32
        )

    def x_copy(which, half):
        return remote(
            sent.at[which, half], got.at[which, half], x_send.at[which, half], x_recv.at[which, half], x_partner
        )

    def partner_part(which, lhs, rhs, half):
        sent[which, half] = product(lhs, rhs, theirs, half)
        x_copy(which, half).start()

    def own_part(which, lhs, rhs, half):
        kept[which, half] = product(lhs, rhs, ours, half)

    def own_chunk(which, lhs, rhs, half, row_z, first):
        rows = pl.ds(pl.multiple_of(row_z * RING * ROWS, ROWS), RING * ROWS)
        value = lax.dot_general(
            lhs[ours, rows], rhs[half, rows], (((0,), (0,)), ((), ())), preferred_element_type=jnp.float32
        )
        kept[which, half] = value if first else kept[which, half] + value

    def out_copy(which, out, turned, half, owner, start):
        block, row_z = (z, y) if turned else (y, z)
        src = rounded.at[which, half, pl.ds(owner * OWNED, OWNED)]
        dst = out.at[:, pl.ds(pl.multiple_of(block * BLOCK + half * HALF, HALF), HALF)]
        recv = out_recv.at[which, block, half]
        itself = (owner == y) & (row_z == z)

        @pl.when(itself)
        def _():
            if start:
                pltpu.make_async_copy(src, dst, recv).start()

        @pl.when(jnp.logical_not(itself))
        def _():
            copy = remote(src, dst, out_send.at[which, half, owner], recv, here(owner, row_z))
            if start:
                copy.start()
            else:
                copy.wait_send()

    def finish(which, out, turned, half):
        x_copy(which, half).wait_recv()
        rounded[which, half] = ((kept[which, half] + got[which, half]) * inverse).astype(jnp.bfloat16)
        for owner in range(RING):
            out_copy(which, out, turned, half, owner, True)

    def drain(which, out, turned):
        @pl.loop(0, 2)
        def _(half):
            x_copy(which, half).wait_send()
            for owner in range(RING):
                out_copy(which, out, turned, half, owner, False)
            for block in range(RING):
                dst = out.at[:, pl.ds(pl.multiple_of(block * BLOCK + half * HALF, HALF), HALF)]
                remote(
                    rounded.at[which, half, pl.ds(0, OWNED)], dst, out_send.at[which, half, 0],
                    out_recv.at[which, block, half], x_partner,
                ).wait_recv()

    def relayed(half, to):
        return remote(
            x_ref.at[:, pl.ds(to * BLOCK + half * HALF, HALF)],
            prev.at[half, pl.ds(pl.multiple_of(slot(z, y) * ROWS, ROWS), ROWS)],
            prev_send.at[half, to], prev_recv.at[half, slot(z, y)], device(1, x_lo, to, z, 0),
        )

    @pl.when(core == 0)
    def _():
        lefts = Flow(place, left, left_send, left_recv, False, (theirs, ours))
        rights = Flow(place, right, right_send, right_recv, True, (0, 1))
        prevs = Flow(place, prev, prev_send, prev_recv, True, (theirs, ours))
        passed = []

        def hand_over(order, index):
            half = lefts.halves[order]
            whole = lefts.piece(order, index)
            to = prev.at[half, pl.ds(pl.multiple_of(index * ROWS, ROWS), ROWS)]
            copy = remote(whole, to, pass_send.at[half, index], prev_recv.at[half, index], other_core)
            copy.start()
            passed.append(copy)

        def rest_left(order):
            for index in lefts.rest():
                lefts.wait(order, index)
                hand_over(order, index)

        def left_own(order, part):
            hand_over(order, lefts.own(order, part))

        def left_relay(order, step, part):
            hand_over(order, lefts.relay(order, step, part))

        lefts.spread(x_ref, 0)
        for part in PIECES:
            left_own(0, part)
        lefts.spread(x_ref, 1)
        rights.spread(x_ref, 0)
        weave(left_relay, 0, left_own, 1)
        rights.spread(x_ref, 1)
        rest_left(0)
        weave(left_relay, 1, rights.own, 0)

        @pl.when(x_hi == 0)
        def _():
            for order in range(2):
                prevs.spread(e_ref, order)

        rest_left(1)
        weave(rights.relay, 0, rights.own, 1)
        rights.wait_rest(0)
        partner_part(0, left, right, 0)
        weave(rights.relay, 1, prevs.own, 0)
        rights.wait_rest(1)
        partner_part(0, left, right, 1)
        weave(prevs.relay, 0, prevs.own, 1)
        own_part(0, left, right, 0)
        prevs.wait_rest(0)
        partner_part(1, prev, left, 0)
        partner_part(1, prev, left, 1)
        for step, part in FORWARD:
            prevs.relay(1, step, part)
        own_part(0, left, right, 1)
        finish(0, d_ref, False, 0)
        for half in range(2):
            own_chunk(1, prev, left, half, z, True)
        finish(0, d_ref, False, 1)
        for step, part in prevs.REST[:4]:
            prevs.wait(1, prevs.index(step, part))
        for half in range(2):
            own_chunk(1, prev, left, half, turn(z, 1), False)
            own_chunk(1, prev, left, half, turn(z, -1), False)
        for step, part in prevs.REST[4:]:
            prevs.wait(1, prevs.index(step, part))
        for half in range(2):
            own_chunk(1, prev, left, half, turn(z, 2), False)
            finish(1, a_ref, True, half)
        drain(0, d_ref, False)
        drain(1, a_ref, True)
        for order in range(2):
            lefts.drain(order)
            rights.drain(order)
            prevs.drain(order, 3)
        for copy in passed:
            copy.wait_send()

        @pl.when(x_hi == 0)
        def _():
            for order in range(2):
                for count in range(3):
                    whole = prevs.piece(order, prevs.mine)
                    half = prevs.halves[order]
                    remote(whole, whole, prev_send.at[half, count], prev_recv.at[half, 0], x_partner).wait_send()

    @pl.when(core == 1)
    def _():
        lefts = Flow(place, left, left_send, left_recv, False, (theirs, ours))
        rights = Flow(place, right, right_send, right_recv, True, (0, 1))
        prevs = Flow(place, prev, prev_send, prev_recv, False, (theirs, ours))

        def wait_prev(order):
            for part in PIECES:
                prevs.wait(order, prevs.index(0, part))
            for step, part in FORWARD:
                prevs.wait(order, prevs.index(step, part))
            prevs.wait_rest(order)

        rights.spread(x_ref, 0)

        @pl.when(x_hi == 0)
        def _():
            for half in range(2):
                for to in range(RING):
                    relayed(half, to).start()

        for part in PIECES:
            rights.own(0, part)
        rights.spread(x_ref, 1)
        lefts.spread(x_ref, 0)
        weave(rights.relay, 0, rights.own, 1)
        lefts.spread(x_ref, 1)
        rights.wait_rest(0)
        wait_prev(0)
        partner_part(1, prev, right, 0)
        weave(rights.relay, 1, lefts.own, 0)
        rights.wait_rest(1)
        partner_part(1, prev, right, 1)
        weave(lefts.relay, 0, lefts.own, 1)
        lefts.wait_rest(0)
        partner_part(0, left, right, 0)
        partner_part(0, left, right, 1)
        for step, part in FORWARD:
            lefts.relay(1, step, part)
        wait_prev(1)
        own_part(1, prev, right, 0)
        finish(1, a_ref, False, 0)
        own_part(1, prev, right, 1)
        finish(1, a_ref, False, 1)
        lefts.wait_rest(1)
        own_part(0, left, right, 0)
        finish(0, d_ref, False, 0)
        own_part(0, left, right, 1)
        finish(0, d_ref, False, 1)
        drain(1, a_ref, False)
        drain(0, d_ref, False)
        for order in range(2):
            lefts.drain(order)
            rights.drain(order)

        @pl.when(x_hi == 0)
        def _():
            for half in range(2):
                for to in range(RING):
                    relayed(half, to).wait_send()


def on_device(factor_rows, entry_rows):
    rows, width = factor_rows.shape[2:]
    tokens = rows * lax.axis_size("dp")
    out = jax.ShapeDtypeStruct((OWNED, width), jnp.bfloat16)
    block = pltpu.VMEM((2, tokens // 2, HALF), jnp.bfloat16)
    part = pltpu.VMEM((2, 2, HALF, HALF), jnp.float32)
    slots = pltpu.SemaphoreType.DMA((2, 16))
    diagonal, adjacent = pl.pallas_call(
        functools.partial(kernel, 1.0 / tokens),
        out_shape=(out, out),
        in_specs=[pl.BlockSpec(memory_space=pl.ANY)] * 2,
        out_specs=[pl.BlockSpec(memory_space=pl.ANY)] * 2,
        scratch_shapes=[block, block, block, part, part, part, pltpu.VMEM((2, 2, HALF, HALF), jnp.bfloat16)]
        + [slots] * 7
        + [
            pltpu.SemaphoreType.DMA((2, 2)),
            pltpu.SemaphoreType.DMA((2, 2)),
            pltpu.SemaphoreType.DMA((2, 2, RING)),
            pltpu.SemaphoreType.DMA((2, RING, 2)),
        ],
        compiler_params=pltpu.CompilerParams(
            collective_id=0, has_side_effects=True, vmem_limit_bytes=60 * 2**20
        ),
        cost_estimate=pl.CostEstimate(flops=4 * BLOCK * BLOCK * tokens // 2, bytes_accessed=2**22, transcendentals=0),
        name="blocks",
    )(factor_rows.reshape(rows, width), entry_rows.reshape(rows, width))
    return diagonal.reshape(1, 1, OWNED, width), adjacent.reshape(1, 1, OWNED, width)


def solution(mesh):
    placed = (P(None, "section", "dp", None), P(None, "dp", None))
    return jax.shard_map(
        on_device,
        mesh=mesh,
        in_specs=placed,
        out_specs=(P(None, "section", "dp", None), P(None, "section", "dp", None)),
        check_vma=False,
    )
```

time: 498 us -> 113 us (0.23)
  the two profiles are of different devices: /device:TPU:59 before, /device:TPU:20 now
where the time goes in v2:
time: 113 us
  Pallas kernels  109 us (96%)
  local copies, waits for them, and re-layouts  2.8 us (2%)
    pallas_call x1, Pallas kernels, on_device(): pl.pallas_call(functools.partial(kernel, 1.0 / tokens), out_shape=(out, o...  109 us
    unnamed x4, local copies, waits for them, and re-layouts  2.8 us

profile of v2, /device:TPU:20, one launch (start us, length us, event | category | flops | bytes accessed | tf_op | source)
XLA Modules:
  0.0 112.8 jit_solution(225364336101153971)
XLA Ops:
  0.6 109.3 %blocks.1 = (bf16[96,3072]{1,0:T(8,128)(2,1)}, bf16[96,3072]{1,0:T(8,128)(2,1)}) custom-call(bf16[192,3072]{1,0:T(8,128)(2,1)} %bitcast.6, bf16[192,3072]{1,0:T(8,128)(2,1)} %bitcast.7), custom_call_target="tpu_custom_call" | custom-call | flops 7247757312 | bytes 4194304 | tf_op jit(solution)/shard_map/blocks/pallas_call | solution.py:402
  110.0 0.0 copy-start
  110.0 2.0 %copy.6 = bf16[1,1,96,3072]{3,2,1,0:T(8,128)(2,1)} copy(bf16[1,1,96,3072]{3,2,1,0:T(8,128)(2,1)} %bitcast.5) | data formatting | bytes 1179648
  111.9 0.0 copy-done
  111.9 0.8 copy.7
Async XLA Ops:
  110.0 2.0 %copy-start = (bf16[96,3072]{1,0:T(8,128)(2,1)S(1)}, bf16[96,3072]{1,0:T(8,128)(2,1)}, u32[]{:S(2)}) copy-start(bf16[96,3072]{1,0:T(8,128)(2,1)} %get-tuple-element.5) | copy-start | bytes 1769476

commit v3 on v2

v3 whole, which is shorter than its diff:
```python
import functools

import jax
import jax.numpy as jnp
from jax import lax
from jax.experimental import pallas as pl
from jax.experimental.pallas import tpu as pltpu
from jax.sharding import PartitionSpec as P

MESH = pl.DeviceIdType.MESH
RING = 4
ROWS = 192
BLOCK = 768
HALF = 384
OWNED = 96
DEPTH = 3
PIECES = (0, 1, 3, 2)
FORWARD = ((-1, 0), (1, 3), (-1, 1), (1, 2))


def device(x_hi, x_lo, y, z, core):
    return (x_hi * 2 + core, z * 8 + x_lo * 4 + y)


def turn(position, by):
    return lax.rem(position + by + RING, RING)


def remote(src, dst, send, recv, target):
    return pltpu.make_async_remote_copy(
        src_ref=src, dst_ref=dst, send_sem=send, recv_sem=recv, device_id=target, device_id_type=MESH
    )


def slot(row_z, row_y):
    return row_z * RING + row_y


class Flow:
    def __init__(self, place, buffer, send, recv, along_z, halves, kept=None):
        self.here, self.y, self.z = place
        self.buffer, self.send, self.recv, self.along_z, self.halves = buffer, send, recv, along_z, halves
        self.kept = halves if kept is None else kept
        self.copies = ([], [])
        self.flying = {1: [], -1: []}
        self.mine = slot(self.z, self.y)

    def piece(self, order, index):
        return self.buffer.at[self.kept[order], pl.ds(pl.multiple_of(index * ROWS, ROWS), ROWS)]

    def columns(self, src, order, block):
        start = pl.multiple_of(block * BLOCK + self.halves[order] * HALF, HALF)
        return src.at[:, pl.ds(start, HALF)]

    def start(self, src, order, index, target):
        half = self.kept[order]
        count = len(self.copies[order])
        copy = remote(src, self.piece(order, index), self.send.at[half, count], self.recv.at[half, index], target)
        copy.start()
        self.copies[order].append(copy)

    def wait(self, order, index):
        whole = self.piece(order, index)
        half = self.kept[order]
        remote(whole, whole, self.send.at[half, 0], self.recv.at[half, index], self.neighbour(1)).wait_recv()

    def spread(self, src, order):
        own = self.y if self.along_z else self.z
        pltpu.make_async_copy(
            self.columns(src, order, own), self.piece(order, self.mine), self.recv.at[self.kept[order], self.mine]
        ).start()
        for step in (1, 3, 2):
            to = turn(own, step)
            target = self.here(to, self.z) if self.along_z else self.here(self.y, to)
            self.start(self.columns(src, order, to), order, self.mine, target)

    def index(self, step, part):
        if self.along_z:
            return slot(turn(self.z, step), turn(self.y, part))
        return slot(turn(self.z, part), turn(self.y, step))

    def neighbour(self, step):
        return self.here(self.y, turn(self.z, step)) if self.along_z else self.here(turn(self.y, step), self.z)

    def push(self, order, index, step):
        flying = self.flying[step]
        if len(flying) == DEPTH:
            past, count = flying.pop(0)
            self.copies[past][count].wait_send()
            self.copies[past][count] = None
        flying.append((order, len(self.copies[order])))
        self.start(self.piece(order, index), order, index, self.neighbour(step))

    def own(self, order, part):
        index = self.index(0, part)
        self.wait(order, index)
        self.push(order, index, 1)
        self.push(order, index, -1)
        return index

    def relay(self, order, step, part):
        index = self.index(step, part)
        self.wait(order, index)
        self.push(order, index, -step)
        return index

    REST = ((-1, 3), (-1, 2), (1, 0), (1, 1), (2, 0), (2, 1), (2, 3), (2, 2))

    def rest(self):
        return [self.index(step, part) for step, part in self.REST]

    def wait_rest(self, order):
        for index in self.rest():
            self.wait(order, index)

    def drain(self, order, first=0):
        for copy in self.copies[order][first:]:
            if copy is not None:
                copy.wait_send()


def weave(relay, behind, own, ahead):
    relay(behind, *FORWARD[0])
    relay(behind, *FORWARD[1])
    own(ahead, 0)
    own(ahead, 1)
    relay(behind, *FORWARD[2])
    relay(behind, *FORWARD[3])
    own(ahead, 3)
    own(ahead, 2)


def kernel(
    inverse, x_ref, e_ref, d_ref, a_ref, left, right, prev, last, staged, sent, got, kept, rounded,
    left_send, left_recv, right_send, right_recv, prev_recv, last_send, last_recv, pass_send, relay_send, relay_recv,
    x_send, x_recv, out_send, out_recv,
):
    section = lax.axis_index("section")
    group = lax.axis_index("dp")
    x_hi, core = section // 2, lax.rem(section, 2)
    z, x_lo, y = group // 8, lax.rem(group // 4, 2), lax.rem(group, 4)

    def here(at_y, at_z):
        return device(x_hi, x_lo, at_y, at_z, core)

    place = (here, y, z)
    theirs, ours = 1 - x_lo, x_lo
    x_partner = device(x_hi, 1 - x_lo, y, z, core)
    other_core = device(x_hi, x_lo, y, z, 1 - core)

    barrier = pltpu.get_barrier_semaphore()

    def greet(target):
        pl.semaphore_signal(barrier, inc=1, device_id=target, device_id_type=MESH)

    for step in range(1, RING):
        greet(here(turn(y, step), z))
        greet(here(y, turn(z, step)))
    greet(x_partner)
    greet(other_core)

    @pl.when(core == 0)
    def _():
        for step in range(RING):
            greet(device(x_hi, x_lo, z, step, 1))

    @pl.when(core == 1)
    def _():
        greet(device(x_hi, 1 - x_lo, y, z, 0))

    @pl.when(x_hi == 1)
    def _():
        greet(device(0, x_lo, y, z, 1))

    expected = 8 + jnp.where(core == 0, 1, 4 + jnp.where(x_hi == 0, 2, 0))
    pl.semaphore_wait(barrier, expected)

    def product(lhs, rhs):
        return lax.dot_general(lhs[...], rhs[...], (((0,), (0,)), ((), ())), preferred_element_type=jnp.float32)

    def x_copy(which, half, at=None, target=None):
        at = which if at is None else at
        target = x_partner if target is None else target
        return remote(
            sent.at[which, half], got.at[at, half], x_send.at[which, half], x_recv.at[at, half], target
        )

    def last_copy(half):
        return x_copy(1, half, 2, device(x_hi, 1 - x_lo, y, z, 1))

    def partner_part(which, lhs, rhs, half):
        sent[which, half] = product(lhs.at[theirs], rhs.at[half])
        x_copy(which, half).start()

    def own_part(which, lhs, rhs, half):
        kept[which, half] = product(lhs.at[ours], rhs.at[half])

    def own_chunk(which, lhs, rhs, half, row_z, first):
        rows = pl.ds(pl.multiple_of(row_z * RING * ROWS, ROWS), RING * ROWS)
        value = product(lhs.at[0, rows], rhs.at[half, rows])
        kept[which, half] = value if first else kept[which, half] + value

    def out_copy(which, out, turned, half, owner, start):
        block, row_z = (z, y) if turned else (y, z)
        src = rounded.at[which, half, pl.ds(owner * OWNED, OWNED)]
        dst = out.at[:, pl.ds(pl.multiple_of(block * BLOCK + half * HALF, HALF), HALF)]
        if turned:
            recv = out_recv.at[1, block, half]
            copy = remote(src, dst, out_send.at[which, half, owner], recv, device(x_hi, x_lo, owner, row_z, 0))
            if start:
                copy.start()
            else:
                copy.wait_send()
            return
        recv = out_recv.at[which, block, half]

        @pl.when(owner == y)
        def _():
            if start:
                pltpu.make_async_copy(src, dst, recv).start()

        @pl.when(owner != y)
        def _():
            copy = remote(src, dst, out_send.at[which, half, owner], recv, here(owner, row_z))
            if start:
                copy.start()
            else:
                copy.wait_send()

    def finish(which, out, turned, half):
        x_copy(which, half).wait_recv() if which < 2 else x_copy(1, half, 2).wait_recv()
        rounded[which, half] = ((kept[which, half] + got[which, half]) * inverse).astype(jnp.bfloat16)
        for owner in range(RING):
            out_copy(which, out, turned, half, owner, True)

    def drain_sends(which, out, turned):
        @pl.loop(0, 2)
        def _(half):
            for owner in range(RING):
                out_copy(which, out, turned, half, owner, False)

    def drain_x(which):
        @pl.loop(0, 2)
        def _(half):
            x_copy(which, half).wait_send()

    def drain_out(which, out):
        @pl.loop(0, 2)
        def _(half):
            for block in range(RING):
                dst = out.at[:, pl.ds(pl.multiple_of(block * BLOCK + half * HALF, HALF), HALF)]
                remote(
                    rounded.at[which, half, pl.ds(0, OWNED)], dst, out_send.at[which, half, 0],
                    out_recv.at[which, block, half], x_partner,
                ).wait_recv()

    def spread_last(lasts):
        @pl.when(x_hi == 0)
        def _():
            lasts.spread(e_ref, 0)

        lasts.copies[0].clear()

        @pl.when(x_hi == 1)
        def _():
            for to in range(RING):
                relayed(core, to).wait_recv()
            lasts.spread(staged, 0)

        lasts.copies[0][:] = [None] * len(lasts.copies[0])

    def drain_last(lasts):
        whole = lasts.piece(0, lasts.mine)
        for count in range(RING - 1):
            remote(whole, whole, last_send.at[0, count], last_recv.at[0, 0], x_partner).wait_send()

    def relayed(to_core, to):
        half = lax.rem(to_core + theirs, 2)
        columns = pl.ds(pl.multiple_of(to * BLOCK + half * HALF, HALF), HALF)
        return remote(
            x_ref.at[:, columns], staged.at[:, columns], relay_send.at[to_core, to], relay_recv.at[to],
            device(1, x_lo, y, z, to_core),
        )

    @pl.when(core == 0)
    def _():
        lefts = Flow(place, left, left_send, left_recv, False, (theirs, ours))
        rights = Flow(place, right, right_send, right_recv, True, (0, 1))
        lasts = Flow(place, last, last_send, last_recv, True, (theirs,), (0,))
        passed = []

        def hand_over(order, index):
            half = lefts.halves[order]
            whole = lefts.piece(order, index)
            to = prev.at[half, pl.ds(pl.multiple_of(index * ROWS, ROWS), ROWS)]
            copy = remote(whole, to, pass_send.at[half, index], prev_recv.at[half, index], other_core)
            copy.start()
            passed.append(copy)

        def rest_left(order):
            for index in lefts.rest():
                lefts.wait(order, index)
                hand_over(order, index)

        def left_own(order, part):
            hand_over(order, lefts.own(order, part))

        def left_relay(order, step, part):
            hand_over(order, lefts.relay(order, step, part))

        lefts.spread(x_ref, 0)
        for part in PIECES:
            left_own(0, part)
        rights.spread(x_ref, 0)
        weave(left_relay, 0, rights.own, 0)
        lefts.spread(x_ref, 1)
        rest_left(0)
        weave(rights.relay, 0, left_own, 1)
        spread_last(lasts)
        rights.wait_rest(0)
        partner_part(0, left, right, 0)
        weave(left_relay, 1, lasts.own, 0)
        rights.spread(x_ref, 1)
        rest_left(1)
        weave(lasts.relay, 0, rights.own, 1)
        own_part(0, left, right, 0)
        lasts.wait_rest(0)
        for half in range(2):
            sent[1, half] = product(last.at[0], left.at[half])
            last_copy(half).start()
        for step, part in FORWARD:
            rights.relay(1, step, part)
        finish(0, d_ref, False, 0)
        rights.wait_rest(1)
        partner_part(0, left, right, 1)
        own_part(0, left, right, 1)
        finish(0, d_ref, False, 1)
        drain_x(0)
        drain_sends(0, d_ref, False)
        lefts.drain(0)
        lefts.drain(1)
        rights.drain(0)
        rights.drain(1)
        lasts.drain(0)
        drain_last(lasts)
        for copy in passed:
            copy.wait_send()
        for half in range(2):
            last_copy(half).wait_send()
        drain_out(0, d_ref)
        drain_out(1, a_ref)

    @pl.when(core == 1)
    def _():
        lefts = Flow(place, left, left_send, left_recv, False, (theirs, ours))
        rights = Flow(place, right, right_send, right_recv, True, (0, 1))
        prevs = Flow(place, prev, left_send, prev_recv, False, (theirs, ours))
        lasts = Flow(place, last, last_send, last_recv, True, (ours,), (0,))

        def wait_prev(order):
            for part in PIECES:
                prevs.wait(order, prevs.index(0, part))
            for step, part in FORWARD:
                prevs.wait(order, prevs.index(step, part))
            prevs.wait_rest(order)

        def relay_last(to_core):
            @pl.when(x_hi == 0)
            def _():
                for to in range(RING):
                    relayed(to_core, to).start()

        rights.spread(x_ref, 0)
        relay_last(0)
        relay_last(1)
        for part in PIECES:
            rights.own(0, part)
        lefts.spread(x_ref, 0)
        weave(rights.relay, 0, lefts.own, 0)
        rights.spread(x_ref, 1)
        rights.wait_rest(0)
        wait_prev(0)
        partner_part(1, prev, right, 0)
        weave(lefts.relay, 0, rights.own, 1)
        lefts.spread(x_ref, 1)
        lefts.wait_rest(0)
        partner_part(0, left, right, 0)
        weave(rights.relay, 1, lefts.own, 1)
        rights.wait_rest(1)
        partner_part(1, prev, right, 1)
        partner_part(0, left, right, 1)
        for step, part in FORWARD:
            lefts.relay(1, step, part)
        spread_last(lasts)
        wait_prev(1)
        own_part(1, prev, right, 0)
        own_part(1, prev, right, 1)
        for part in PIECES:
            lasts.own(0, part)
        finish(1, a_ref, False, 0)
        finish(1, a_ref, False, 1)
        for step, part in FORWARD[:2]:
            lasts.relay(0, step, part)
        lefts.wait_rest(1)
        own_part(0, left, right, 0)
        for step, part in FORWARD[2:]:
            lasts.relay(0, step, part)
        own_part(0, left, right, 1)
        for half in range(2):
            own_chunk(2, last, prev, half, z, True)
        finish(0, d_ref, False, 0)
        for step, part in lasts.REST[:4]:
            lasts.wait(0, lasts.index(step, part))
        for half in range(2):
            own_chunk(2, last, prev, half, turn(z, 1), False)
            own_chunk(2, last, prev, half, turn(z, -1), False)
        finish(0, d_ref, False, 1)
        for step, part in lasts.REST[4:]:
            lasts.wait(0, lasts.index(step, part))
        for half in range(2):
            own_chunk(2, last, prev, half, turn(z, 2), False)
            finish(2, a_ref, True, half)
        drain_x(0)
        drain_x(1)
        drain_sends(0, d_ref, False)
        drain_sends(1, a_ref, False)
        drain_sends(2, a_ref, True)
        for order in range(2):
            lefts.drain(order)
            rights.drain(order)
        lasts.drain(0)
        drain_last(lasts)

        @pl.when(x_hi == 0)
        def _():
            for to_core in range(2):
                for to in range(RING):
                    relayed(to_core, to).wait_send()

        drain_out(1, a_ref)
        drain_out(0, d_ref)


def on_device(factor_rows, entry_rows):
    rows, width = factor_rows.shape[2:]
    tokens = rows * lax.axis_size("dp")
    out = jax.ShapeDtypeStruct((OWNED, width), jnp.bfloat16)
    block = pltpu.VMEM((2, tokens // 2, HALF), jnp.bfloat16)
    part = pltpu.VMEM((3, 2, HALF, HALF), jnp.float32)
    slots = pltpu.SemaphoreType.DMA((2, 16))
    diagonal, adjacent = pl.pallas_call(
        functools.partial(kernel, 1.0 / tokens),
        out_shape=(out, out),
        in_specs=[pl.BlockSpec(memory_space=pl.ANY)] * 2,
        out_specs=[pl.BlockSpec(memory_space=pl.ANY)] * 2,
        scratch_shapes=[
            block, block, block, pltpu.VMEM((1, tokens // 2, HALF), jnp.bfloat16),
            pltpu.VMEM((rows, width), jnp.bfloat16),
            pltpu.VMEM((2, 2, HALF, HALF), jnp.float32), part, part, pltpu.VMEM((3, 2, HALF, HALF), jnp.bfloat16),
        ]
        + [slots] * 8
        + [
            pltpu.SemaphoreType.DMA((2, RING)),
            pltpu.SemaphoreType.DMA((RING,)),
            pltpu.SemaphoreType.DMA((2, 2)),
            pltpu.SemaphoreType.DMA((3, 2)),
            pltpu.SemaphoreType.DMA((3, 2, RING)),
            pltpu.SemaphoreType.DMA((2, RING, 2)),
        ],
        compiler_params=pltpu.CompilerParams(
            collective_id=0, has_side_effects=True, vmem_limit_bytes=60 * 2**20
        ),
        cost_estimate=pl.CostEstimate(flops=4 * BLOCK * BLOCK * tokens // 2, bytes_accessed=2**22, transcendentals=0),
        name="blocks",
    )(factor_rows.reshape(rows, width), entry_rows.reshape(rows, width))
    return diagonal.reshape(1, 1, OWNED, width), adjacent.reshape(1, 1, OWNED, width)


def solution(mesh):
    placed = (P(None, "section", "dp", None), P(None, "dp", None))
    return jax.shard_map(
        on_device,
        mesh=mesh,
        in_specs=placed,
        out_specs=(P(None, "section", "dp", None), P(None, "section", "dp", None)),
        check_vma=False,
    )
```

time: 113 us -> 103 us (0.912)
  Pallas kernels: 109 us -> 99.4 us
    pallas_call x1, Pallas kernels: 109 us -> 99.4 us  [on_device(): pl.pallas_call(functools.partial(kernel, 1.0 / tokens), out_shape=(out, o...]
where the time goes in v3:
time: 103 us
  Pallas kernels  99.4 us (97%)
  local copies, waits for them, and re-layouts  2.8 us (3%)
    pallas_call x1, Pallas kernels, on_device(): pl.pallas_call(functools.partial(kernel, 1.0 / tokens), out_shape=(out, o...  99.4 us
    unnamed x4, local copies, waits for them, and re-layouts  2.8 us

profile of v3, /device:TPU:20, one launch (start us, length us, event | category | flops | bytes accessed | tf_op | source)
XLA Modules:
  0.0 102.8 jit_solution(1731863234840939107)
XLA Ops:
  0.6 99.4 %blocks.1 = (bf16[96,3072]{1,0:T(8,128)(2,1)}, bf16[96,3072]{1,0:T(8,128)(2,1)}) custom-call(bf16[192,3072]{1,0:T(8,128)(2,1)} %bitcast.6, bf16[192,3072]{1,0:T(8,128)(2,1)} %bitcast.7), custom_call_target="tpu_custom_call" | custom-call | flops 7247757312 | bytes 4194304 | tf_op jit(solution)/shard_map/blocks/pallas_call | solution.py:451
  100.0 0.0 copy-start
  100.0 2.0 %copy.6 = bf16[1,1,96,3072]{3,2,1,0:T(8,128)(2,1)} copy(bf16[1,1,96,3072]{3,2,1,0:T(8,128)(2,1)} %bitcast.5) | data formatting | bytes 1179648
  102.0 0.0 copy-done
  102.0 0.8 copy.7
Async XLA Ops:
  100.0 2.0 %copy-start = (bf16[96,3072]{1,0:T(8,128)(2,1)S(1)}, bf16[96,3072]{1,0:T(8,128)(2,1)}, u32[]{:S(2)}) copy-start(bf16[96,3072]{1,0:T(8,128)(2,1)} %get-tuple-element.5) | copy-start | bytes 1769476

commit v4 on v3

--- a/solution.py
+++ b/solution.py
@@ -178,12 +178,29 @@
     def product(lhs, rhs):
         return lax.dot_general(lhs[...], rhs[...], (((0,), (0,)), ((), ())), preferred_element_type=jnp.float32)
 
+    class Pair:
+        def __init__(self, *copies):
+            self.copies = copies
+
+        def start(self):
+            for copy in self.copies:
+                copy.start()
+
+        def wait_send(self):
+            for copy in self.copies:
+                copy.wait_send()
+
     def x_copy(which, half, at=None, target=None):
         at = which if at is None else at
         target = x_partner if target is None else target
-        return remote(
-            sent.at[which, half], got.at[at, half], x_send.at[which, half], x_recv.at[at, half], target
-        )
+        halves = [pl.ds(0, HALF // 2), pl.ds(HALF // 2, HALF // 2)]
+        return Pair(*(
+            remote(
+                sent.at[which, half, rows], got.at[at, half, rows],
+                x_send.at[which, half, n], x_recv.at[at, half, n], target,
+            )
+            for n, rows in enumerate(halves)
+        ))
 
     def last_copy(half):
         return x_copy(1, half, 2, device(x_hi, 1 - x_lo, y, z, 1))
@@ -228,10 +245,14 @@
                 copy.wait_send()
 
     def finish(which, out, turned, half):
-        x_copy(which, half).wait_recv() if which < 2 else x_copy(1, half, 2).wait_recv()
-        rounded[which, half] = ((kept[which, half] + got[which, half]) * inverse).astype(jnp.bfloat16)
-        for owner in range(RING):
-            out_copy(which, out, turned, half, owner, True)
+        arriving = x_copy(min(which, 1), half, which).copies
+        for n in range(2):
+            arriving[n].wait_recv()
+            rows = pl.ds(n * HALF // 2, HALF // 2)
+            total = kept[which, half, rows] + got[which, half, rows]
+            rounded[which, half, rows] = (total * inverse).astype(jnp.bfloat16)
+            for owner in (2 * n, 2 * n + 1):
+                out_copy(which, out, turned, half, owner, True)
 
     def drain_sends(which, out, turned):
         @pl.loop(0, 2)
@@ -323,28 +344,29 @@
         rights.spread(x_ref, 1)
         rest_left(1)
         weave(lasts.relay, 0, rights.own, 1)
-        own_part(0, left, right, 0)
+        rights.relay(1, -1, 0)
         lasts.wait_rest(0)
+        rights.relay(1, -1, 1)
         for half in range(2):
             sent[1, half] = product(last.at[0], left.at[half])
             last_copy(half).start()
-        for step, part in FORWARD:
-            rights.relay(1, step, part)
-        finish(0, d_ref, False, 0)
-        rights.wait_rest(1)
-        partner_part(0, left, right, 1)
-        own_part(0, left, right, 1)
-        finish(0, d_ref, False, 1)
-        drain_x(0)
-        drain_sends(0, d_ref, False)
+            rights.relay(1, 1, 3 - half)
+        own_part(0, left, right, 0)
         lefts.drain(0)
         lefts.drain(1)
         rights.drain(0)
+        for copy in passed:
+            copy.wait_send()
+        rights.wait_rest(1)
+        partner_part(0, left, right, 1)
+        finish(0, d_ref, False, 0)
+        own_part(0, left, right, 1)
+        finish(0, d_ref, False, 1)
         rights.drain(1)
         lasts.drain(0)
         drain_last(lasts)
-        for copy in passed:
-            copy.wait_send()
+        drain_x(0)
+        drain_sends(0, d_ref, False)
         for half in range(2):
             last_copy(half).wait_send()
         drain_out(0, d_ref)
@@ -415,30 +437,35 @@
             own_chunk(2, last, prev, half, turn(z, 1), False)
             own_chunk(2, last, prev, half, turn(z, -1), False)
         finish(0, d_ref, False, 1)
+        for order in range(2):
+            lefts.drain(order)
+            rights.drain(order)
+
+        @pl.when(x_hi == 0)
+        def _():
+            for to_core in range(2):
+                for to in range(RING):
+                    relayed(to_core, to).wait_send()
+
+        drain_x(0)
+        drain_x(1)
+        drain_sends(0, d_ref, False)
+        drain_sends(1, a_ref, False)
         for step, part in lasts.REST[4:]:
             lasts.wait(0, lasts.index(step, part))
         for half in range(2):
             own_chunk(2, last, prev, half, turn(z, 2), False)
             finish(2, a_ref, True, half)
-        drain_x(0)
-        drain_x(1)
-        drain_sends(0, d_ref, False)
-        drain_sends(1, a_ref, False)
-        drain_sends(2, a_ref, True)
-        for order in range(2):
-            lefts.drain(order)
-            rights.drain(order)
         lasts.drain(0)
         drain_last(lasts)
-
-        @pl.when(x_hi == 0)
-        def _():
-            for to_core in range(2):
-                for to in range(RING):
-                    relayed(to_core, to).wait_send()
-
+        drain_sends(2, a_ref, True)
         drain_out(1, a_ref)
         drain_out(0, d_ref)
+
+
+def copies(first, second, first_out, second_out):
+    first_out[...] = first[...]
+    second_out[...] = second[...]
 
 
 def on_device(factor_rows, entry_rows):
@@ -462,8 +489,8 @@
         + [
             pltpu.SemaphoreType.DMA((2, RING)),
             pltpu.SemaphoreType.DMA((RING,)),
-            pltpu.SemaphoreType.DMA((2, 2)),
-            pltpu.SemaphoreType.DMA((3, 2)),
+            pltpu.SemaphoreType.DMA((2, 2, 2)),
+            pltpu.SemaphoreType.DMA((3, 2, 2)),
             pltpu.SemaphoreType.DMA((3, 2, RING)),
             pltpu.SemaphoreType.DMA((2, RING, 2)),
         ],
@@ -473,6 +500,7 @@
         cost_estimate=pl.CostEstimate(flops=4 * BLOCK * BLOCK * tokens // 2, bytes_accessed=2**22, transcendentals=0),
         name="blocks",
     )(factor_rows.reshape(rows, width), entry_rows.reshape(rows, width))
+    diagonal, adjacent = pl.pallas_call(copies, out_shape=(out, out), name="outputs")(diagonal, adjacent)
     return diagonal.reshape(1, 1, OWNED, width), adjacent.reshape(1, 1, OWNED, width)
 
 

time: 103 us -> 102 us (level)
  local copies, waits for them, and re-layouts: 2.8 us -> 0 us
  Pallas kernels: 99.4 us -> 101 us
    unnamed x4 -> x0, local copies, waits for them, and re-layouts: 2.8 us -> none
    pallas_call x0 -> x1, Pallas kernels: none -> 2.29 us  [on_device(): pl.pallas_call(copies, out_shape=(out, out), name='outputs')]
where the time goes in v4:
time: 102 us
  Pallas kernels  101 us (99%)
    pallas_call x1, Pallas kernels, on_device(): pl.pallas_call(functools.partial(kernel, 1.0 / tokens), out_shape=(out, o...  98.6 us
    pallas_call x1, Pallas kernels, on_device(): pl.pallas_call(copies, out_shape=(out, out), name='outputs')  2.29 us

profile of v4, /device:TPU:20, one launch (start us, length us, event | category | flops | bytes accessed | tf_op | source)
XLA Modules:
  0.0 101.5 jit_solution(8303071913505293601)
XLA Ops:
  0.6 98.6 %blocks.1 = (bf16[96,3072]{1,0:T(8,128)(2,1)}, bf16[96,3072]{1,0:T(8,128)(2,1)}) custom-call(bf16[192,3072]{1,0:T(8,128)(2,1)} %bitcast.4, bf16[192,3072]{1,0:T(8,128)(2,1)} %bitcast.5), custom_call_target="tpu_custom_call" | custom-call | flops 7247757312 | bytes 4194304 | tf_op jit(solution)/shard_map/blocks/pallas_call | solution.py:478
  99.2 2.3 %outputs.1 = (bf16[96,3072]{1,0:T(8,128)(2,1)}, bf16[96,3072]{1,0:T(8,128)(2,1)}) custom-call(bf16[96,3072]{1,0:T(8,128)(2,1)} %get-tuple-element.6.first, bf16[96,3072]{1,0:T(8,128)(2,1)} %get-tuple-element.7.second), custom_call_target="tpu_custom_call" | custom-call | tf_op jit(solution)/shard_map/outputs/pallas_call | solution.py:503

commit v5 on v4

--- a/solution.py
+++ b/solution.py
@@ -13,7 +13,7 @@
 BLOCK = 768
 HALF = 384
 OWNED = 96
-DEPTH = 3
+DEPTH = 16
 PIECES = (0, 1, 3, 2)
 FORWARD = ((-1, 0), (1, 3), (-1, 1), (1, 2))
 
@@ -122,10 +122,10 @@
 def weave(relay, behind, own, ahead):
     relay(behind, *FORWARD[0])
     relay(behind, *FORWARD[1])
+    relay(behind, *FORWARD[2])
+    relay(behind, *FORWARD[3])
     own(ahead, 0)
     own(ahead, 1)
-    relay(behind, *FORWARD[2])
-    relay(behind, *FORWARD[3])
     own(ahead, 3)
     own(ahead, 2)
 

time: 102 us -> 99 us (0.971); the launches traced: 102 us -> 97.4 us
  Pallas kernels: 101 us -> 96.8 us
    pallas_call x1, Pallas kernels: 98.6 us -> 94.5 us  [on_device(): pl.pallas_call(functools.partial(kernel, 1.0 / tokens), out_shape=(out, o...]
where the time goes in v5:
time: 99 us; the launch traced here: 97.4 us
  Pallas kernels  96.8 us (98%)
    pallas_call x1, Pallas kernels, on_device(): pl.pallas_call(functools.partial(kernel, 1.0 / tokens), out_shape=(out, o...  94.5 us
    pallas_call x1, Pallas kernels, on_device(): pl.pallas_call(copies, out_shape=(out, out), name='outputs')  2.29 us

profile of v5, /device:TPU:20, one launch (start us, length us, event | category | flops | bytes accessed | tf_op | source)
XLA Modules:
  0.0 97.4 jit_solution(17915551832475465006)
XLA Ops:
  0.6 94.5 %blocks.1 = (bf16[96,3072]{1,0:T(8,128)(2,1)}, bf16[96,3072]{1,0:T(8,128)(2,1)}) custom-call(bf16[192,3072]{1,0:T(8,128)(2,1)} %bitcast.4, bf16[192,3072]{1,0:T(8,128)(2,1)} %bitcast.5), custom_call_target="tpu_custom_call" | custom-call | flops 7247757312 | bytes 4194304 | tf_op jit(solution)/shard_map/blocks/pallas_call | solution.py:478
  95.1 2.3 %outputs.1 = (bf16[96,3072]{1,0:T(8,128)(2,1)}, bf16[96,3072]{1,0:T(8,128)(2,1)}) custom-call(bf16[96,3072]{1,0:T(8,128)(2,1)} %get-tuple-element.6.first, bf16[96,3072]{1,0:T(8,128)(2,1)} %get-tuple-element.7.second), custom_call_target="tpu_custom_call" | custom-call | tf_op jit(solution)/shard_map/outputs/pallas_call | solution.py:503
